TPU v7x, 256 devices: a whole 4x4x8 slice. The times are simulated.
256 devices in a mesh: leaf: 8 (over y, core), branch: 32 (over x, z).
Axes of the slice: x: 4, y: 4, z: 8, core: 2. Of those that a mesh axis runs over, the one named last changes fastest.
Arguments:
- queries: bfloat16 [65536, 2560], P(('leaf', 'branch')), parts along dimension 0, may hold values from -4.5 to 4.5
- branch_key_rows: bfloat16 [65536, 512], P(('leaf', 'branch')), parts along dimension 0, may hold values from -4.5 to 4.5
- branch_value_rows: bfloat16 [65536, 512], P(('leaf', 'branch')), parts along dimension 0, may hold values from -4.5 to 4.5
- prefix_keys: bfloat16 [4096, 512], P(('leaf', 'branch')), parts along dimension 0, may hold values from -4.5 to 4.5
- prefix_value_rows: bfloat16 [4096, 512], P(('leaf', 'branch')), parts along dimension 0, may hold values from -4.5 to 4.5
- cotangent: bfloat16 [65536, 2560], P(('leaf', 'branch')), parts along dimension 0, may hold values from -6 to 6
- rewards: int32 [256], P(('leaf', 'branch')), parts along dimension 0, may hold values from 0 to 29, as said below
- lengths: int32 [256], P(('leaf', 'branch')), parts along dimension 0, may hold values from 32 to 256, as said below
- parents: int32 [65536], P(('leaf', 'branch')), parts along dimension 0, may hold values from -1 to 254, as said below
Outputs:
- attended: bfloat16 [65536, 2560], P(('leaf', 'branch')), parts along dimension 0
- grad_queries: bfloat16 [65536, 2560], P(('leaf', 'branch')), parts along dimension 0
- grad_branch_keys: bfloat16 [65536, 512], P(('leaf', 'branch')), parts along dimension 0
- grad_branch_values: bfloat16 [65536, 512], P(('leaf', 'branch')), parts along dimension 0
- grad_prefix_keys: float32 [4096, 512], P(('leaf', 'branch')), parts along dimension 0
- grad_prefix_values: float32 [4096, 512], P(('leaf', 'branch')), parts along dimension 0
There are 8 independent parts, one for each index of `leaf`. A program takes and returns all parts, laid end to end along the dimension named above; each array names one. Nothing has to cross between parts.
Inputs may be any that keep to these rules, and one draw needn't show every extreme that they name: `rewards`: branch b draws its reward from 0 to 9 + 20 * b // 31; the last branch of every tree has the reward 29. `lengths`: some branch of every tree has all 256 slots valid. `parents`: each token's parent is an earlier token of its own branch, given by its position in the branch; the first token of a branch has -1, and the last slot's parent is the slot before it.
All inputs are finite; a program needn't handle non-finite values.
Results may differ from a plain program's by a relative error of at most 0.012.
Values may be sent and summed in bfloat16 or wider, within the bound.
No kernel may reach another device: no remote copies, remote signals or barrier semaphores. Data moves between devices by JAX's collectives and lax.ppermute only.
A program may use at most 128 MiB of HBM per device.

v0:
```python
import jax
import jax.numpy as jnp
from jax import lax
from jax.sharding import PartitionSpec as P

HEAD_SIZE = 128


MASKED = -1e30


def ancestry(parents, length_rows):
    places = jnp.arange(length_rows, dtype=jnp.int32)
    one_step = (parents[:, None] == places[None, :]) | (places[:, None] == places[None, :])
    closure = one_step.astype(jnp.bfloat16)
    for squaring in range(max(1, (length_rows - 1).bit_length())):
        counted = jnp.dot(closure, closure, preferred_element_type=jnp.float32)
        closure = jnp.minimum(counted, 1.0).astype(jnp.bfloat16)
    return closure > 0.5


def contract(grouped, key_rows):
    blocks = key_rows.reshape(key_rows.shape[0], grouped.shape[1], grouped.shape[3])
    return jnp.einsum("tgjd,ngd->gjtn", grouped, blocks, preferred_element_type=jnp.float32)


def mixture(weights, value_rows, grouped):
    blocks = value_rows.reshape(value_rows.shape[0], grouped.shape[1], grouped.shape[3])
    return jnp.einsum("gjtn,ngd->gjtd", weights, blocks, preferred_element_type=jnp.float32)


def transposed(weights, grouped):
    product = jnp.einsum("gjtn,tgjd->ngd", weights, grouped, preferred_element_type=jnp.float32)
    return product.reshape(product.shape[0], -1)


def on_device(
    queries,
    branch_key_rows,
    branch_value_rows,
    prefix_keys,
    prefix_value_rows,
    cotangent,
    rewards,
    lengths,
    parents,
):
    length_rows = queries.shape[0]
    groups = branch_key_rows.shape[1] // HEAD_SIZE
    per_group = queries.shape[1] // (groups * HEAD_SIZE)
    score_scale = HEAD_SIZE ** (-0.5)
    grouped = queries.reshape(length_rows, groups, per_group, HEAD_SIZE)
    tree_mask = ancestry(parents, length_rows)
    score_own = jnp.where(
        tree_mask[None, None], contract(grouped, branch_key_rows) * score_scale, MASKED
    )
    top_own = score_own.max(-1)
    total_own = jnp.sum(jnp.exp(score_own - top_own[..., None]), -1)
    whole_keys, whole_values = (
        lax.all_gather(prefix_keys, "branch", axis=0, tiled=True),
        lax.all_gather(prefix_value_rows, "branch", axis=0, tiled=True),
    )
    score_pre = contract(grouped, whole_keys) * score_scale
    row_top = jnp.maximum(top_own, score_pre.max(-1))
    row_total = total_own * jnp.exp(top_own - row_top) + jnp.sum(
        jnp.exp(score_pre - row_top[..., None]), -1
    )
    log_total = row_top + jnp.log(row_total)
    prob_pre = jnp.exp(score_pre - log_total[..., None])
    weight_pre = prob_pre.astype(jnp.bfloat16)
    out_pre = mixture(weight_pre, whole_values, grouped)
    prob_own = jnp.exp(score_own - log_total[..., None])
    weight_own = prob_own.astype(jnp.bfloat16)
    outputs = out_pre + mixture(weight_own, branch_value_rows, grouped)
    valid_rows = (jnp.arange(length_rows, dtype=jnp.int32) < lengths[0]).astype(jnp.float32)
    flat_out = outputs.transpose(2, 0, 1, 3).reshape(length_rows, -1)
    attended = (flat_out * valid_rows[:, None]).astype(jnp.bfloat16)
    reward_float = rewards.astype(jnp.float32)
    reward_sum = lax.psum(reward_float, "branch")
    advantage = (reward_float[0] - reward_sum[0] / lax.axis_size("branch")) / 10.0
    weighted = (cotangent.astype(jnp.float32) * advantage * valid_rows[:, None]).astype(
        jnp.bfloat16
    )
    weight_grp = weighted.reshape(length_rows, groups, per_group, HEAD_SIZE)
    delta_rows = jnp.sum(weight_grp.astype(jnp.float32).transpose(1, 2, 0, 3) * outputs, -1)
    dscore_own = (
        prob_own * (contract(weight_grp, branch_value_rows) - delta_rows[..., None])
    ).astype(jnp.bfloat16)
    dscore_pre = (prob_pre * (contract(weight_grp, whole_values) - delta_rows[..., None])).astype(
        jnp.bfloat16
    )
    grad_rows = score_scale * (
        mixture(dscore_own, branch_key_rows, grouped) + mixture(dscore_pre, whole_keys, grouped)
    )
    grad_queries = grad_rows.transpose(2, 0, 1, 3).reshape(length_rows, -1).astype(jnp.bfloat16)
    grad_branch_keys = (score_scale * transposed(dscore_own, grouped)).astype(jnp.bfloat16)
    grad_branch_values = transposed(weight_own, weight_grp).astype(jnp.bfloat16)
    shard_rows = prefix_keys.shape[0]
    summed = lax.psum(
        jnp.concatenate(
            [score_scale * transposed(dscore_pre, grouped), transposed(weight_pre, weight_grp)], 1
        ),
        "branch",
    )
    prefix_grad = lax.dynamic_slice_in_dim(
        summed, lax.axis_index("branch") * shard_rows, shard_rows, 0
    )
    key_width = prefix_keys.shape[1]
    return (
        attended,
        grad_queries,
        grad_branch_keys,
        grad_branch_values,
        prefix_grad[:, :key_width],
        prefix_grad[:, key_width:],
    )


def solution(mesh):
    return jax.shard_map(
        on_device,
        mesh=mesh,
        in_specs=(
            P(("leaf", "branch"), None),
            P(("leaf", "branch"), None),
            P(("leaf", "branch"), None),
            P(("leaf", "branch"), None),
            P(("leaf", "branch"), None),
            P(("leaf", "branch"), None),
            P(("leaf", "branch")),
            P(("leaf", "branch")),
            P(("leaf", "branch")),
        ),
        out_specs=(
            P(("leaf", "branch"), None),
            P(("leaf", "branch"), None),
            P(("leaf", "branch"), None),
            P(("leaf", "branch"), None),
            P(("leaf", "branch"), None),
            P(("leaf", "branch"), None),
        ),
        check_vma=False,
    )
```

profile of v0, /device:TPU:8, one launch (start us, length us, event | category | flops | bytes accessed | tf_op | source)
XLA Modules:
  0.0 390.0 jit_solution(6280450182298642638)
XLA Ops:
  7.2 0.0 copy-start.18
  7.2 0.0 all-reduce.2.cloned.1.call-start
  8.5 78.2 %psum.14 = f32[1]{0:T(128)} all-reduce(f32[1]{0:T(128)S(6)} %convert_element_type.97), channel_id=1, replica_groups=mesh['leaf'=8,'branch'=32] {'branch'}, use_global_device_ids=true, to_apply=%region_4.5 | all-reduce | flops 1 | bytes 8 | tf_op jit(solution)/shard_map/psum | solution.py:79
  87.4 1.4 fusion.16
  88.7 0.4 fusion.18
  89.2 0.4 fusion.20
  89.6 0.5 fusion.23
  90.1 0.2 copy.81
  90.3 1.0 reshape.86
  91.3 0.2 copy.120
  91.5 0.0 copy-start.14
  91.5 1.1 reshape.88
  92.6 0.0 copy-start.16
  92.6 46.8 %all_gather.6 = bf16[512,512]{1,0:T(8,128)(2,1)S(1)} all-gather(bf16[16,512]{1,0:T(8,128)(2,1)} %param.12), channel_id=1, replica_groups=mesh['leaf'=8,'branch'=32] {'branch'}, dimensions={0}, use_global_device_ids=true | all-gather | bytes 540672 | tf_op jit(solution)/shard_map/all_gather | solution.py:60
  139.5 0.2 copy.77
  139.7 0.0 copy-done.18
  139.7 0.0 copy-start.7
  139.7 48.6 %all_gather.7 = bf16[512,512]{1,0:T(8,128)(2,1)S(1)} all-gather(bf16[16,512]{1,0:T(8,128)(2,1)S(1)} %copy-done.18), channel_id=1, replica_groups=mesh['leaf'=8,'branch'=32] {'branch'}, dimensions={0}, use_global_device_ids=true | all-gather | bytes 540672 | tf_op jit(solution)/shard_map/all_gather | solution.py:61
  188.3 0.2 copy.84
  188.6 0.0 copy-start.9
  188.6 1.8 copy.78
  190.4 0.0 copy-start.4
  190.4 1.6 bitcast_reduce_fusion
  191.9 0.0 copy-done.14
  192.0 0.0 copy-done.7
  192.0 0.0 copy-done.4
  192.0 1.0 fusion.9
  193.0 1.1 exponential_reduce_fusion
  194.1 1.7 fusion.3
  195.9 0.0 copy-done.9
  195.9 0.0 copy-done
  196.0 2.3 fusion.26
  198.3 1.5 convolution_add_fusion
  199.8 2.3 copy.88
  202.1 4.2 %multiply_convert_fusion.1 = (bf16[256,2560]{1,0:T(8,128)(2,1)}, bf16[256,2560]{1,0:T(8,128)(2,1)}) fusion(bf16[256,2560]{1,0:T(8,128)(2,1)} %param.14, f32[]{:T(128)} %bitcast.13, f32[256]{0:T(256)S(1)} %compare_convert_fusion, f32[256,2560]{1,0:T(8,128)} %copy.88), kind=kLoop, calls=%fused_computation.21 | loop fusion | flops 3932160 | bytes 6554628 | tf_op jit(solution)/shard_map/convert_element_type | solution.py:81
  206.3 1.7 copy.89
  208.0 0.0 slice-start.1
  208.0 2.3 fusion.10
  210.3 0.0 slice-start.2
  210.3 0.0 copy-start.10
  210.3 7.2 %fusion.24 = f32[4,128,512,1]{2,1,3,0:T(8,128)} fusion(bf16[256,4,5,128]{0,3,2,1:T(8,128)(2,1)S(1)} %bitcast.135, f32[4,512,256,5]{2,1,3,0:T(8,128)} %copy-done, f32[4,5,256]{2,1,0:T(8,128)S(1)} %log_add_fusion), kind=kOutput, calls=%fused_computation.49 | convolution fusion | flops 678952960 | bytes 12865536 | tf_op jit(solution)/shard_map/gjtn,tgjd->ngd/dot_general | solution.py:33
  217.5 0.0 slice-done
  217.5 3.0 fusion.1
  220.5 2.3 copy-done.2
  222.8 0.0 copy-done.5
  222.8 2.8 fusion.11
  225.6 1.6 copy.103
  227.2 1.3 copy.104
  228.5 2.7 pad_maximum_fusion
  231.2 0.0 all-reduce.2.cloned.1.call-update
  231.3 0.0 copy-start.17
  231.3 3.8 fusion.14
  235.1 0.8 copy.107
  235.9 4.4 %fusion.7 = bf16[4,5,256,256]{2,3,1,0:T(8,128)(2,1)S(1)} fusion(f32[4,256,256,5]{2,1,3,0:T(8,128)} %copy-done.1, f32[4,5,256]{2,1,0:T(8,128)S(1)} %fusion.10, f32[4,5,256]{2,1,0:T(8,128)S(1)} %log_add_fusion, pred[256,256]{0,1:T(8,128)(4,1)S(1)} %copy.81, bf16[256,4,5,128]{0,3,2,1:T(8,128)(2,1)S(1)} %bitcast.138, bf16[256,4,128,1]{2,1,0,3:T(4,128)(2,1)S(1)} %bitcast.152), kind=kOutput, calls=%fused_computation.12 | convolution fusion | flops 343408640 | bytes 9543680 | tf_op jit(solution)/shard_map/tgjd,ngd->gjtn/dot_general | solution.py:24
  240.4 0.0 copy-done.6
  240.4 0.0 copy-start.12
  240.4 1.0 fusion.13
  241.4 0.5 copy-done.12
  241.9 0.8 copy.106
  242.7 3.6 fusion.52
  246.3 0.6 multiply_convert_fusion
  246.9 1.6 copy.105
  248.5 133.3 %all-reduce.2.cloned.1.call-done = f32[512,1024]{1,0:T(8,128)} async-done(((f32[512,1024]{1,0:T(8,128)}), f32[512,1024]{1,0:T(8,128)}) %all-reduce.2.cloned.1.call-update) | async-done | bytes 2097168 | tf_op jit(solution)/shard_map/psum | solution.py:99
  381.8 1.4 fusion.51
  (26 shorter events, 0.1 us)
Async XLA Ops:
  7.2 132.5 %copy-start.18 = (bf16[16,512]{1,0:T(8,128)(2,1)S(1)}, bf16[16,512]{1,0:T(8,128)(2,1)}, u32[]{:S(2)}) copy-start(bf16[16,512]{1,0:T(8,128)(2,1)} %param.13) | copy-start | bytes 49156
  7.2 374.6 %all-reduce.2.cloned.1.call-start = ((), (), s32[]{:S(2)}) async-start(), calls=%async_computation | async-start | bytes 4194304 | tf_op jit(solution)/shard_map/psum | solution.py:99
  91.5 100.5 %copy-start.14 = (bf16[256,4,128,1]{0,2,3,1:T(8,128)(2,1)}, bf16[256,4,128,1]{0,2,3,1:T(8,128)(2,1)S(1)}, u32[]{:S(2)}) copy-start(bf16[256,4,128,1]{0,2,3,1:T(8,128)(2,1)S(1)} %copy.120) | copy-start | bytes 786436
  92.6 105.7 %copy-start.16 = (bf16[256,4,128]{2,1,0:T(4,128)(2,1)}, bf16[256,4,128]{2,1,0:T(4,128)(2,1)S(1)}, u32[]{:S(2)}) copy-start(bf16[256,4,128]{2,1,0:T(4,128)(2,1)S(1)} %reshape.88) | copy-start | bytes 786436
  139.7 52.3 %copy-start.7 = (bf16[512,512]{0,1:T(8,128)(2,1)}, bf16[512,512]{0,1:T(8,128)(2,1)S(1)}, u32[]{:S(2)}) copy-start(bf16[512,512]{0,1:T(8,128)(2,1)S(1)} %copy.77) | copy-start | bytes 1572868
  188.6 7.4 %copy-start.9 = (bf16[512,512]{0,1:T(8,128)(2,1)}, bf16[512,512]{0,1:T(8,128)(2,1)S(1)}, u32[]{:S(2)}) copy-start(bf16[512,512]{0,1:T(8,128)(2,1)S(1)} %copy.84) | copy-start | bytes 1572868
  190.4 1.6 copy-start.4
  192.0 4.0 %copy-start = (f32[4,512,256,5]{2,1,3,0:T(8,128)}, f32[4,512,256,5]{2,1,3,0:T(8,128)S(1)}, u32[]{:S(2)}) copy-start(f32[4,512,256,5]{2,1,3,0:T(8,128)S(1)} %get-tuple-element.31) | copy-start | bytes 31457284
  193.0 5.3 %copy-start.1 = (f32[4,256,256,5]{2,1,3,0:T(8,128)}, f32[4,256,256,5]{2,1,3,0:T(8,128)S(1)}, u32[]{:S(2)}) copy-start(f32[4,256,256,5]{2,1,3,0:T(8,128)S(1)} %get-tuple-element.29) | copy-start | bytes 15728644
  199.8 6.4 %copy-start.3 = (f32[4,5,256,128]{2,3,1,0:T(8,128)}, f32[4,5,256,128]{2,3,1,0:T(8,128)S(1)}, u32[]{:S(2)}) copy-start(f32[4,5,256,128]{2,3,1,0:T(8,128)S(1)} %convolution_add_fusion) | copy-start | bytes 7864324
  206.3 11.2 %slice-start = ((s8[10485760]{0:T(1024)(128)(4,1)}), s8[2097152]{0:T(1024)(128)(4,1)S(1)}, s32[]{:S(2)}) async-start(s8[10485760]{0:T(1024)(128)(4,1)} %bitcast.131), calls=%async_computation.1 | async-start | bytes 4194304
  208.0 9.5 %slice-start.1 = ((s8[10485760]{0:T(1024)(128)(4,1)}), s8[4194304]{0:T(1024)(128)(4,1)S(1)}, s32[]{:S(2)}) async-start(s8[10485760]{0:T(1024)(128)(4,1)} %bitcast.131), calls=%async_computation.2 | async-start | bytes 8388608
  210.3 7.2 %slice-start.2 = ((s8[10485760]{0:T(1024)(128)(4,1)}), s8[4194304]{0:T(1024)(128)(4,1)S(1)}, s32[]{:S(2)}) async-start(s8[10485760]{0:T(1024)(128)(4,1)} %bitcast.131), calls=%async_computation.3 | async-start | bytes 8388608
  210.3 7.2 %copy-start.10 = (bf16[512,512]{0,1:T(8,128)(2,1)S(1)}, bf16[512,512]{0,1:T(8,128)(2,1)}, u32[]{:S(2)}) copy-start(bf16[512,512]{0,1:T(8,128)(2,1)} %copy-done.9) | copy-start | bytes 1572868
  217.5 5.3 %copy-start.5 = (bf16[256,2560]{0,1:T(8,128)(2,1)S(1)}, bf16[256,2560]{0,1:T(8,128)(2,1)}, u32[]{:S(2)}) copy-start(bf16[256,2560]{0,1:T(8,128)(2,1)} %copy-done.4) | copy-start | bytes 3932164
  220.5 2.3 copy-start.2
  222.8 4.4 %copy-start.11 = (f32[4,128,512,1]{2,1,3,0:T(8,128)S(1)}, f32[4,128,512,1]{2,1,3,0:T(8,128)}, u32[]{:S(2)}) copy-start(f32[4,128,512,1]{2,1,3,0:T(8,128)} %fusion.24) | copy-start | bytes 3145732
  231.3 4.7 %copy-start.17 = (bf16[256,4,128]{2,1,0:T(4,128)(2,1)S(1)}, bf16[256,4,128]{2,1,0:T(4,128)(2,1)}, u32[]{:S(2)}) copy-start(bf16[256,4,128]{2,1,0:T(4,128)(2,1)} %copy-done.16) | copy-start | bytes 786436
  235.9 4.4 %copy-start.6 = (bf16[256,2560]{0,1:T(8,128)(2,1)S(1)}, bf16[256,2560]{0,1:T(8,128)(2,1)}, u32[]{:S(2)}) copy-start(bf16[256,2560]{0,1:T(8,128)(2,1)} %copy-done.4) | copy-start | bytes 3932164
  235.9 6.8 %copy-start.8 = (bf16[512,512]{0,1:T(8,128)(2,1)S(1)}, bf16[512,512]{0,1:T(8,128)(2,1)}, u32[]{:S(2)}) copy-start(bf16[512,512]{0,1:T(8,128)(2,1)} %copy-done.7) | copy-start | bytes 1572868
  240.4 1.5 copy-start.12
  241.9 4.5 %copy-start.15 = (bf16[256,4,128,1]{0,2,3,1:T(8,128)(2,1)S(1)}, bf16[256,4,128,1]{0,2,3,1:T(8,128)(2,1)}, u32[]{:S(2)}) copy-start(bf16[256,4,128,1]{0,2,3,1:T(8,128)(2,1)} %copy-done.14) | copy-start | bytes 786436
  242.7 3.6 copy-start.13
Sparse Core Ops, SparseCore 0:
  231.4 150.3 all-reduce.1
where the time goes:
time: 391 us; the launch traced here: 390 us
  blocking collectives  174 us (45%)
  waiting for transfers between devices  133 us (34%)
  matrix products  35.4 us (9%)
  local copies, waits for them, and re-layouts  19.1 us (5%)
  between operations  16.4 us (4%)
  other arithmetic  12.1 us (3%)
    psum x1, waiting for transfers between devices, on_device(): lax.psum(jnp.concatenate([score_scale * transposed(dscore_pre, grouped),...  133 us
    psum x1, blocking collectives, on_device(): reward_sum = lax.psum(reward_float, 'branch')  78.2 us
    all_gather x1, blocking collectives, on_device(): lax.all_gather(prefix_value_rows, 'branch', axis=0, tiled=True)  48.6 us
    all_gather x1, blocking collectives, on_device(): lax.all_gather(prefix_keys, 'branch', axis=0, tiled=True)  46.8 us
    dot_general x4, matrix products, transposed(): jnp.einsum('gjtn,tgjd->ngd', weights, grouped, preferred_element_type=jnp...  14.8 us
    dot_general x4, matrix products, contract(): jnp.einsum('tgjd,ngd->gjtn', grouped, blocks, preferred_element_type=jnp....  9.95 us
    dot_general x4, matrix products, mixture(): jnp.einsum('gjtn,ngd->gjtd', weights, blocks, preferred_element_type=jnp....  8.01 us
    unnamed x48, local copies, waits for them, and re-layouts  7.95 us
  transfers between devices with their start and end apart: 1, of which 1 were waited for; matrix products, arithmetic and copies ran while one was open for 4% of the time, Pallas kernels for 0%

commit v1 on v0

v1 whole, which is shorter than its diff:
```python
import jax
import jax.numpy as jnp
from jax import lax
from jax.experimental import pallas as pl
from jax.experimental.pallas import tpu as pltpu
from jax.sharding import PartitionSpec as P

HEAD = 128
SCALE = HEAD ** (-0.5)
LOG2E = 1.4426950408889634
MASKED = -1e30
BF = jnp.bfloat16
F32 = jnp.float32
LIMIT = 48 * 1024 * 1024


def nt(a, b):
    return lax.dot_general(a, b, (((1,), (1,)), ((), ())), preferred_element_type=F32)


def nn(a, b):
    return lax.dot_general(a, b, (((1,), (0,)), ((), ())), preferred_element_type=F32)


def tn(a, b):
    return lax.dot_general(a, b, (((0,), (0,)), ((), ())), preferred_element_type=F32)


def head(ref, j):
    return ref[:, j * HEAD : (j + 1) * HEAD]


def ancestry_bias(parents_row, rows):
    child = lax.broadcasted_iota(jnp.int32, (rows, rows), 1)
    place = lax.broadcasted_iota(jnp.int32, (rows, rows), 0)
    step = (parents_row == place) | (child == place)
    closure = jnp.where(step, 1.0, 0.0).astype(BF)
    rounds = max(1, (rows - 1).bit_length())
    for _ in range(rounds - 1):
        closure = jnp.where(nn(closure, closure) > 0.5, 1.0, 0.0).astype(BF)
    counted = lax.dot_general(closure, closure, (((0,), (1,)), ((), ())), preferred_element_type=F32)
    return jnp.where(counted > 0.5, 0.0, MASKED)


def own_forward(per_group, par_ref, q_ref, k_ref, v_ref, p_ref, o_ref, st_ref, bias):
    @pl.when(pl.program_id(0) == 0)
    def _():
        bias[...] = ancestry_bias(par_ref[...], bias.shape[0])

    keys, values = k_ref[...], v_ref[...]
    for j in range(per_group):
        s = nt(head(q_ref, j), keys) * (SCALE * LOG2E) + bias[...]
        m = jnp.max(s, axis=1, keepdims=True)
        p = jnp.exp2(s - m)
        st_ref[0, :, j : j + 1] = m
        st_ref[0, :, 8 + j : 9 + j] = jnp.sum(p, axis=1, keepdims=True)
        pb = p.astype(BF)
        p_ref[j] = pb
        o_ref[:, j * HEAD : (j + 1) * HEAD] = nn(pb, values)


def prefix_forward(
    per_group, branches, len_ref, q_ref, cot_ref, o_ref, st_ref, *rest
):
    chunks = [rest[3 * c : 3 * c + 3] for c in range(4)]
    att_ref, w_ref, wr_ref, qr_ref, p_ref, ds_ref, st2_ref = rest[12:]
    rows = q_ref.shape[0]
    keys = jnp.concatenate([c[0][...] for c in chunks], axis=0)
    values = jnp.concatenate([c[1][...] for c in chunks], axis=0)
    total = sum(jnp.sum(c[2][...].astype(F32), axis=0, keepdims=True) for c in chunks)
    mine = chunks[0][2][0:16, :].astype(F32)[0:1, :]
    advantage = (mine - total / (branches * 16)) / 10.0
    valid = lax.broadcasted_iota(jnp.int32, (rows, HEAD), 0) < len_ref[0]
    factor = jnp.where(valid, advantage, 0.0)
    for j in range(per_group):
        cols = slice(j * HEAD, (j + 1) * HEAD)
        q = q_ref[:, cols]
        w = (cot_ref[:, cols].astype(F32) * factor).astype(BF)
        w_ref[:, cols] = w
        wf = w.astype(F32)
        s = nt(q, keys) * (SCALE * LOG2E)
        m_own = st_ref[0, :, j : j + 1]
        l_own = st_ref[0, :, 8 + j : 9 + j]
        m = jnp.maximum(m_own, jnp.max(s, axis=1, keepdims=True))
        p = jnp.exp2(s - m)
        a_own = jnp.exp2(m_own - m)
        r = 1.0 / (l_own * a_own + jnp.sum(p, axis=1, keepdims=True))
        pb = p.astype(BF)
        p_ref[j] = pb
        out = (nn(pb, values) + o_ref[:, cols] * a_own) * r
        att_ref[:, cols] = jnp.where(valid, out, 0.0).astype(BF)
        delta = jnp.sum(wf * out, axis=1, keepdims=True)
        st2_ref[0, :, j : j + 1] = delta
        st2_ref[0, :, 8 + j : 9 + j] = a_own * r
        st2_ref[0, :, 16 + j : 17 + j] = r
        ds_ref[j] = (p * (nt(w, values) - delta)).astype(BF)
        wr_ref[:, cols] = (wf * r).astype(BF)
        qr_ref[:, cols] = (q.astype(F32) * (r * SCALE)).astype(BF)


def stack(ref, per_group):
    return jnp.concatenate([head(ref, j) for j in range(per_group)], axis=0)


def prefix_grads(per_group, p_ref, ds_ref, qr_ref, wr_ref, g_ref):
    n = p_ref.shape[2]
    rows = p_ref.shape[0] * p_ref.shape[1]
    g_ref[:, :HEAD] = tn(ds_ref[...].reshape(rows, n), stack(qr_ref, per_group)).astype(g_ref.dtype)
    g_ref[:, HEAD:] = tn(p_ref[...].reshape(rows, n), stack(wr_ref, per_group)).astype(g_ref.dtype)


def own_backward(per_group, q_ref, w_ref, k_ref, v_ref, p_ref, ds_ref, st2_ref, c0, c1, c2, c3, dq_ref, dk_ref, dv_ref):
    keys, values = k_ref[...], v_ref[...]
    pre = jnp.concatenate([c[...] for c in (c0, c1, c2, c3)], axis=0)
    dk = jnp.zeros(dk_ref.shape, F32)
    dv = jnp.zeros(dv_ref.shape, F32)
    for j in range(per_group):
        cols = slice(j * HEAD, (j + 1) * HEAD)
        q, w = q_ref[:, cols], w_ref[:, cols]
        delta = st2_ref[0, :, j : j + 1]
        r_own = st2_ref[0, :, 8 + j : 9 + j]
        r = st2_ref[0, :, 16 + j : 17 + j]
        pb = p_ref[j]
        ds = (pb.astype(F32) * (nt(w, values) - delta)).astype(BF)
        dq = (nn(ds_ref[j], pre) * r + nn(ds, keys) * r_own) * SCALE
        dq_ref[:, cols] = dq.astype(BF)
        dk += tn(ds, (q.astype(F32) * (r_own * SCALE)).astype(BF))
        dv += tn(pb, (w.astype(F32) * r_own).astype(BF))
    dk_ref[...] = dk.astype(BF)
    dv_ref[...] = dv.astype(BF)


def exchange(x, bits):
    return lax.ppermute(x, "branch", [(i, i ^ bits) for i in range(lax.axis_size("branch"))])


def on_device(queries, own_keys, own_values, prefix_keys, prefix_values, cotangent, rewards, lengths, parents):
    rows, width = queries.shape
    groups = own_keys.shape[1] // HEAD
    per_group = width // (groups * HEAD)
    gw = per_group * HEAD
    heads = groups * per_group
    shard = prefix_keys.shape[0]
    branches = lax.axis_size("branch")
    npre = shard * branches
    half = groups * HEAD
    params = pltpu.CompilerParams(vmem_limit_bytes=LIMIT, dimension_semantics=("arbitrary",))
    S = jax.ShapeDtypeStruct

    def cols(n, w):
        return pl.BlockSpec((n, w), lambda g: (0, g))

    def per(n, m):
        return pl.BlockSpec((per_group, n, m), lambda g: (g, 0, 0))

    stat = pl.BlockSpec((1, rows, HEAD), lambda g: (g, 0, 0))

    packed = jnp.concatenate(
        [prefix_keys, prefix_values, jnp.broadcast_to(rewards.astype(BF)[:, None], (shard, HEAD))], axis=1
    )
    got = jnp.concatenate([packed, exchange(packed, 6)], axis=0)
    got = jnp.concatenate([got] + [exchange(got, b) for b in (1, 2, 3)], axis=0)
    chunks = [got] + [exchange(got, b * 8) for b in (1, 2, 3)]
    chunk_rows = got.shape[0]

    p_own, o_own, st = pl.pallas_call(
        lambda *refs: own_forward(per_group, *refs),
        grid=(groups,),
        out_shape=(S((heads, rows, rows), BF), S((rows, width), F32), S((groups, rows, HEAD), F32)),
        in_specs=[pl.BlockSpec((1, rows), lambda g: (0, 0)), cols(rows, gw), cols(rows, HEAD), cols(rows, HEAD)],
        out_specs=(per(rows, rows), cols(rows, gw), stat),
        scratch_shapes=[pltpu.VMEM((rows, rows), F32)],
        compiler_params=params,
        cost_estimate=pl.CostEstimate(flops=4 * heads * rows * rows * HEAD * 2, bytes_accessed=8 << 20, transcendentals=heads * rows * rows),
        name="own_forward",
    )(parents.reshape(1, rows), queries, own_keys, own_values)

    def chunk_specs():
        return [
            pl.BlockSpec((chunk_rows, HEAD), lambda g: (0, g)),
            pl.BlockSpec((chunk_rows, HEAD), lambda g: (0, groups + g)),
            pl.BlockSpec((chunk_rows, HEAD), lambda g: (0, 2 * groups)),
        ]

    attended, w, wr, qr, p_pre, ds_pre, st2 = pl.pallas_call(
        lambda *refs: prefix_forward(per_group, branches, *refs),
        grid=(groups,),
        out_shape=(
            S((rows, width), BF),
            S((rows, width), BF),
            S((rows, width), BF),
            S((rows, width), BF),
            S((heads, rows, npre), BF),
            S((heads, rows, npre), BF),
            S((groups, rows, HEAD), F32),
        ),
        in_specs=[pl.BlockSpec(memory_space=pltpu.SMEM), cols(rows, gw), cols(rows, gw), cols(rows, gw), stat]
        + [s for _ in chunks for s in chunk_specs()],
        out_specs=(cols(rows, gw),) * 4 + (per(rows, npre),) * 2 + (stat,),
        compiler_params=params,
        cost_estimate=pl.CostEstimate(flops=6 * heads * rows * npre * HEAD, bytes_accessed=16 << 20, transcendentals=heads * rows * npre),
        name="prefix_forward",
    )(lengths, queries, cotangent, o_own, st, *[c for c in chunks for _ in range(3)])

    def grads_of(c):
        return pl.pallas_call(
            lambda *refs: prefix_grads(per_group, *refs),
            grid=(groups,),
            out_shape=S((chunk_rows, 2 * half), BF),
            in_specs=[pl.BlockSpec((per_group, rows, chunk_rows), lambda g: (g, 0, c))] * 2 + [cols(rows, gw)] * 2,
            out_specs=cols(chunk_rows, 2 * HEAD),
            compiler_params=params,
            cost_estimate=pl.CostEstimate(flops=4 * heads * rows * chunk_rows * HEAD, bytes_accessed=5 << 20, transcendentals=0),
            name=f"prefix_grads_{c}",
        )(p_pre, ds_pre, qr, wr)

    sent = {c: exchange(grads_of(c), c * 8) for c in (2, 1, 3)}

    dq, dk, dv = pl.pallas_call(
        lambda *refs: own_backward(per_group, *refs),
        grid=(groups,),
        out_shape=(S((rows, width), BF), S((rows, half), BF), S((rows, half), BF)),
        in_specs=[cols(rows, gw), cols(rows, gw), cols(rows, HEAD), cols(rows, HEAD), per(rows, rows), per(rows, npre), stat]
        + [pl.BlockSpec((chunk_rows, HEAD), lambda g: (0, g))] * 4,
        out_specs=(cols(rows, gw), cols(rows, HEAD), cols(rows, HEAD)),
        compiler_params=params,
        cost_estimate=pl.CostEstimate(flops=4 * heads * rows * (npre + 3 * rows) * HEAD, bytes_accessed=12 << 20, transcendentals=0),
        name="own_backward",
    )(queries, w, own_keys, own_values, p_own, ds_pre, st2, *chunks)

    def add(parts):
        return sum(p.astype(F32) for p in parts)

    mine = add([grads_of(0)] + [sent[c] for c in (2, 1, 3)]).astype(BF)
    part = mine.reshape(4, 2 * shard, 2 * half)
    mine = add([part[0]] + [exchange(part[b], b) for b in (1, 2, 3)]).astype(BF)
    mine = add([mine[:shard], exchange(mine[shard:], 6)])
    final = mine.reshape(shard, groups, 2, HEAD)
    return (
        attended,
        dq,
        dk,
        dv,
        final[:, :, 0].reshape(shard, half),
        final[:, :, 1].reshape(shard, half),
    )


def solution(mesh):
    split = P(("leaf", "branch"), None)
    line = P(("leaf", "branch"))
    return jax.shard_map(
        on_device,
        mesh=mesh,
        in_specs=(split,) * 6 + (line,) * 3,
        out_specs=(split,) * 6,
        check_vma=False,
    )
```

time: 391 us -> 108 us (0.28)
  blocking collectives: 174 us -> 0 us
  waiting for transfers between devices: 133 us -> 17.7 us
  Pallas kernels: 0 us -> 53.6 us
  matrix products: 35.4 us -> 0 us
  starting transfers between devices: 0.04 us -> 25.1 us
  between operations: 16.4 us -> 2.09 us
  local copies, waits for them, and re-layouts: 19.1 us -> 6.45 us
  other arithmetic: 12.1 us -> 1.7 us
    psum x1 -> x0, waiting for transfers between devices: 133 us -> none  [on_device(): lax.psum(jnp.concatenate([score_scale * transposed(dscore_pre, grouped),...]
    all_gather x2 -> x0, blocking collectives: 95.5 us -> none  [the longest x1 48.6 us: on_device(): lax.all_gather(prefix_value_rows, 'branch', axis=0, tiled=True)]
    psum x1 -> x0, blocking collectives: 78.2 us -> none  [on_device(): reward_sum = lax.psum(reward_float, 'branch')]
    pallas_call x0 -> x7, Pallas kernels: none -> 53.6 us  [the longest x1 24.2 us: on_device(): pl.pallas_call(lambda *refs: prefix_forward(per_group, branches, *refs),...]
    dot_general x16 -> x0, matrix products: 35.4 us -> none  [the longest x4 14.8 us: transposed(): jnp.einsum('gjtn,tgjd->ngd', weights, grouped, preferred_element_type=jnp...]
    ppermute x0 -> x14, starting transfers between devices: none -> 25.1 us  [exchange(): lax.ppermute(x, 'branch', [(i, i ^ bits) for i in range(lax.axis_size('br...]
    ppermute x0 -> x14, waiting for transfers between devices: none -> 17.7 us  [exchange(): lax.ppermute(x, 'branch', [(i, i ^ bits) for i in range(lax.axis_size('br...]
    reshape x5 -> x1, local copies, waits for them, and re-layouts: 5.87 us -> 0.07 us  [on_device(): final = mine.reshape(shard, groups, 2, HEAD)]
  transfers between devices with their start and end apart: 1 -> 14, of which waited for: 1 -> 8; matrix products, arithmetic and copies ran while one was open for 4% -> 0% of each run, Pallas kernels for 0% -> 18%
where the time goes in v1:
time: 108 us; the launch traced here: 107 us
  Pallas kernels  53.6 us (50%)
  starting transfers between devices  25.1 us (23%)
  waiting for transfers between devices  17.7 us (16%)
  local copies, waits for them, and re-layouts  6.45 us (6%)
  between operations  2.09 us (2%)
  other arithmetic  1.7 us (2%)
    ppermute x14, starting transfers between devices, exchange(): lax.ppermute(x, 'branch', [(i, i ^ bits) for i in range(lax.axis_size('br...  25.1 us
    pallas_call x1, Pallas kernels, on_device(): pl.pallas_call(lambda *refs: prefix_forward(per_group, branches, *refs),...  24.2 us
    ppermute x14, waiting for transfers between devices, exchange(): lax.ppermute(x, 'branch', [(i, i ^ bits) for i in range(lax.axis_size('br...  17.7 us
    pallas_call x4, Pallas kernels, grads_of(): pl.pallas_call(lambda *refs: prefix_grads(per_group, *refs), grid=(groups...  13.9 us
    pallas_call x1, Pallas kernels, on_device(): pl.pallas_call(lambda *refs: own_backward(per_group, *refs), grid=(groups...  9.02 us
    pallas_call x1, Pallas kernels, on_device(): pl.pallas_call(lambda *refs: own_forward(per_group, *refs), grid=(groups,...  6.41 us
    unnamed x19, local copies, waits for them, and re-layouts  5.54 us
  transfers between devices with their start and end apart: 14, of which 8 were waited for; matrix products, arithmetic and copies ran while one was open for 0% of the time, Pallas kernels for 18%

profile of v1, /device:TPU:8, one launch (start us, length us, event | category | flops | bytes accessed | tf_op | source)
XLA Modules:
  0.0 106.7 jit_solution(15685458371049826784)
XLA Ops:
  1.3 0.7 pad_maximum_fusion.1
  2.0 6.3 %collective-permute-start = (bf16[16,1152]{1,0:T(8,128)(2,1)S(1)}, bf16[16,1152]{1,0:T(8,128)(2,1)S(1)}, u32[]{:S(2)}, u32[]{:S(2)}) collective-permute-start(bf16[16,1152]{1,0:T(8,128)(2,1)S(1)} %get-tuple-element.37), channel_id=1, source_target_pairs={{0,6},{1,7},{2,4},{3,5},{4,2},{5,3},{6,0},{7,1},{8,14},{9,15},{10,... | collective-permute-start | bytes 110600 | tf_op jit(solution)/shard_map/ppermute | solution.py:134
  8.3 1.9 %collective-permute-done = bf16[16,1152]{1,0:T(8,128)(2,1)S(1)} collective-permute-done((bf16[16,1152]{1,0:T(8,128)(2,1)S(1)}, bf16[16,1152]{1,0:T(8,128)(2,1)S(1)}, u32[]{:S(2)}, u32[]{:S(2)}) %collective-permute-start) | collective-permute-done | bytes 36896 | tf_op jit(solution)/shard_map/ppermute | solution.py:134
  10.3 0.7 pad_maximum_fusion
  11.0 2.5 %collective-permute-start.3 = (bf16[32,1152]{1,0:T(8,128)(2,1)S(1)}, bf16[32,1152]{1,0:T(8,128)(2,1)S(1)}, u32[]{:S(2)}, u32[]{:S(2)}) collective-permute-start(bf16[32,1152]{1,0:T(8,128)(2,1)S(1)} %pad_maximum_fusion), channel_id=1, source_target_pairs={{0,3},{1,2},{2,1},{3,0},{4,7},{5,6},{6,5},{7,4},{8,11},{9,10},{10,... | collective-permute-start | bytes 221192 | tf_op jit(solution)/shard_map/ppermute | solution.py:134
  13.5 0.0 collective-permute-start.2
  13.5 1.9 %collective-permute-start.1 = (bf16[32,1152]{1,0:T(8,128)(2,1)S(1)}, bf16[32,1152]{1,0:T(8,128)(2,1)S(1)}, u32[]{:S(2)}, u32[]{:S(2)}) collective-permute-start(bf16[32,1152]{1,0:T(8,128)(2,1)S(1)} %pad_maximum_fusion), channel_id=1, source_target_pairs={{0,1},{1,0},{2,3},{3,2},{4,5},{5,4},{6,7},{7,6},{8,9},{9,8},{10,11... | collective-permute-start | bytes 221192 | tf_op jit(solution)/shard_map/ppermute | solution.py:134
  15.4 3.1 %collective-permute-done.1 = bf16[32,1152]{1,0:T(8,128)(2,1)S(1)} collective-permute-done((bf16[32,1152]{1,0:T(8,128)(2,1)S(1)}, bf16[32,1152]{1,0:T(8,128)(2,1)S(1)}, u32[]{:S(2)}, u32[]{:S(2)}) %collective-permute-start.1) | collective-permute-done | bytes 73760 | tf_op jit(solution)/shard_map/ppermute | solution.py:134
  18.5 1.4 %collective-permute-done.2 = bf16[32,1152]{1,0:T(8,128)(2,1)S(1)} collective-permute-done((bf16[32,1152]{1,0:T(8,128)(2,1)S(1)}, bf16[32,1152]{1,0:T(8,128)(2,1)S(1)}, u32[]{:S(2)}, u32[]{:S(2)}) %collective-permute-start.2) | collective-permute-done | bytes 73760 | tf_op jit(solution)/shard_map/ppermute | solution.py:134
  19.9 0.0 collective-permute-done.3
  19.9 2.8 %collective-permute-start.6 = (bf16[128,1152]{1,0:T(8,128)(2,1)S(1)}, bf16[128,1152]{1,0:T(8,128)(2,1)S(1)}, u32[]{:S(2)}, u32[]{:S(2)}) collective-permute-start(bf16[128,1152]{1,0:T(8,128)(2,1)S(1)} %constant_dynamic-update-slice_fusion.refs_5_.refs_6_.refs_7_), channel_id=1, source_target_pairs={{0,24},{1,25},{2,26},{3,27},{4,28},{5,29},{6,30},{7,31},{8,16},{9,... | collective-permute-start | bytes 884744 | tf_op jit(solution)/shard_map/ppermute | solution.py:134
  22.8 0.8 collective-permute-start.5
  23.6 0.5 collective-permute-start.4
  24.8 0.0 copy-start
  24.8 1.3 %copy-done = bf16[256,2560]{1,0:T(8,128)(2,1)S(1)} copy-done((bf16[256,2560]{1,0:T(8,128)(2,1)S(1)}, bf16[256,2560]{1,0:T(8,128)(2,1)}, u32[]{:S(2)}) %copy-start) | copy-done | bytes 1310744
  26.1 0.0 copy-start.3
  26.1 0.9 copy-done.3
  27.1 0.0 copy-start.5
  27.1 0.9 copy-done.5
  28.0 0.0 copy-start.7
  28.0 0.7 copy-done.7
  28.7 6.4 %own_forward.1 = (bf16[20,256,256]{2,1,0:T(8,128)(2,1)S(1)}, f32[256,2560]{1,0:T(8,128)}, f32[4,256,128]{2,1,0:T(8,128)S(1)}) custom-call(s32[1,256]{1,0:T(1,128)S(1)} %bitcast.8, bf16[256,2560]{1,0:T(8,128)(2,1)S(1)} %copy-done, bf16[256,512]{1,0:T(8,128)(2,1)S(1)} %copy-done.3, bf16[256,512]{1,0:T(8,128)(2,1)S(1)} %copy-done.5), custom_call_target="tpu_custom_call" | custom-call | flops 1342177280 | bytes 8388608 | tf_op jit(solution)/shard_map/own_forward/pallas_call | solution.py:166
  35.1 0.0 copy-start.2
  35.1 1.6 %copy-done.2 = bf16[20,256,256]{2,1,0:T(8,128)(2,1)} copy-done((bf16[20,256,256]{2,1,0:T(8,128)(2,1)}, bf16[20,256,256]{2,1,0:T(8,128)(2,1)S(1)}, u32[]{:S(2)}) %copy-start.2) | copy-done | bytes 2621464
  36.7 0.0 collective-permute-done.6.refs_14_.refs_15_.refs_16_.refs_10_
  36.7 0.0 collective-permute-done.5.refs_11_.refs_12_.refs_13_.refs_9_
  36.7 0.0 collective-permute-done.4.refs_8_.refs_9_.refs_10_
  36.7 24.2 %prefix_forward.1 = (bf16[256,2560]{1,0:T(8,128)(2,1)}, bf16[256,2560]{1,0:T(8,128)(2,1)S(1)}, bf16[256,2560]{1,0:T(8,128)(2,1)S(1)}, bf16[256,2560]{1,0:T(8,128...) custom-call(s32[1]{0:T(128)S(6)} %copy.24.refs_0_, ...), custom_call_target="tpu_custom_call" | custom-call | flops 2013265920 | bytes 16777216 | tf_op jit(solution)/shard_map/prefix_forward/pallas_call | solution.py:185
  60.9 3.5 %prefix_grads_3.1 = bf16[128,1024]{1,0:T(8,128)(2,1)S(1)} custom-call(bf16[20,256,512]{2,1,0:T(8,128)(2,1)} %get-tuple-element.29.refs_0_, bf16[20,256,512]{2,1,0:T(8,128)(2,1)} %get-tuple-element.24.refs_5_.refs_1_, bf16[256,2560]{1,0:T(8,128)(2,1)S(1)} %get-tuple-element.30.refs_2_, bf16[256,2560]{1,0:T(8,128)(2,1)S(1)} %get-tuple-element.31.refs_3_), custom_call_target="tpu_custom_call" | custom-call | flops 335544320 | bytes 5242880 | tf_op jit(solution)/shard_map/prefix_grads_3/pallas_call | solution.py:206
  64.4 3.5 %prefix_grads_1.1 = bf16[128,1024]{1,0:T(8,128)(2,1)S(1)} custom-call(bf16[20,256,512]{2,1,0:T(8,128)(2,1)} %get-tuple-element.29.refs_0_, bf16[20,256,512]{2,1,0:T(8,128)(2,1)} %get-tuple-element.24.refs_5_.refs_1_, bf16[256,2560]{1,0:T(8,128)(2,1)S(1)} %get-tuple-element.30.refs_2_, bf16[256,2560]{1,0:T(8,128)(2,1)S(1)} %get-tuple-element.31.refs_3_), custom_call_target="tpu_custom_call" | custom-call | flops 335544320 | bytes 5242880 | tf_op jit(solution)/shard_map/prefix_grads_1/pallas_call | solution.py:206
  67.9 3.5 %prefix_grads_2.1 = bf16[128,1024]{1,0:T(8,128)(2,1)S(1)} custom-call(bf16[20,256,512]{2,1,0:T(8,128)(2,1)} %get-tuple-element.29.refs_0_, bf16[20,256,512]{2,1,0:T(8,128)(2,1)} %get-tuple-element.24.refs_5_.refs_1_, bf16[256,2560]{1,0:T(8,128)(2,1)S(1)} %get-tuple-element.30.refs_2_, bf16[256,2560]{1,0:T(8,128)(2,1)S(1)} %get-tuple-element.31.refs_3_), custom_call_target="tpu_custom_call" | custom-call | flops 335544320 | bytes 5242880 | tf_op jit(solution)/shard_map/prefix_grads_2/pallas_call | solution.py:206
  71.4 3.1 %collective-permute-start.7 = (bf16[128,1024]{1,0:T(8,128)(2,1)S(1)}, bf16[128,1024]{1,0:T(8,128)(2,1)S(1)}, u32[]{:S(2)}, u32[]{:S(2)}) collective-permute-start(bf16[128,1024]{1,0:T(8,128)(2,1)S(1)} %prefix_grads_2.1), channel_id=1, source_target_pairs={{0,16},{1,17},{2,18},{3,19},{4,20},{5,21},{6,22},{7,23},{8,24},{9,... | collective-permute-start | bytes 786440 | tf_op jit(solution)/shard_map/ppermute | solution.py:134
  74.5 0.6 collective-permute-start.8
  75.1 0.5 collective-permute-start.9
  75.7 3.5 %prefix_grads_0.1 = bf16[128,1024]{1,0:T(8,128)(2,1)S(1)} custom-call(bf16[20,256,512]{2,1,0:T(8,128)(2,1)} %get-tuple-element.29.refs_0_, bf16[20,256,512]{2,1,0:T(8,128)(2,1)} %get-tuple-element.24.refs_5_.refs_1_, bf16[256,2560]{1,0:T(8,128)(2,1)S(1)} %get-tuple-element.30.refs_2_, bf16[256,2560]{1,0:T(8,128)(2,1)S(1)} %get-tuple-element.31.refs_3_), custom_call_target="tpu_custom_call" | custom-call | flops 335544320 | bytes 5242880 | tf_op jit(solution)/shard_map/prefix_grads_0/pallas_call | solution.py:206
  79.1 0.0 copy-start.1
  79.1 0.0 copy-start.4
  79.2 0.0 copy-start.6
  79.2 3.1 %collective-permute-done.7 = bf16[128,1024]{1,0:T(8,128)(2,1)S(1)} collective-permute-done((bf16[128,1024]{1,0:T(8,128)(2,1)S(1)}, bf16[128,1024]{1,0:T(8,128)(2,1)S(1)}, u32[]{:S(2)}, u32[]{:S(2)}) %collective-permute-start.7) | collective-permute-done | bytes 262176 | tf_op jit(solution)/shard_map/ppermute | solution.py:134
  82.2 3.3 %collective-permute-done.8 = bf16[128,1024]{1,0:T(8,128)(2,1)S(1)} collective-permute-done((bf16[128,1024]{1,0:T(8,128)(2,1)S(1)}, bf16[128,1024]{1,0:T(8,128)(2,1)S(1)}, u32[]{:S(2)}, u32[]{:S(2)}) %collective-permute-start.8) | collective-permute-done | bytes 262176 | tf_op jit(solution)/shard_map/ppermute | solution.py:134
  85.5 0.0 collective-permute-done.9
  85.5 0.2 add_convert_fusion
  85.7 0.1 collective-permute-start.10
  85.8 2.0 %collective-permute-start.12 = (bf16[32,1024]{1,0:T(8,128)(2,1)S(1)}, bf16[32,1024]{1,0:T(8,128)(2,1)S(1)}, u32[]{:S(2)}, u32[]{:S(2)}) collective-permute-start(bf16[32,1024]{1,0:T(8,128)(2,1)S(1)} %get-tuple-element.35), channel_id=1, source_target_pairs={{0,3},{1,2},{2,1},{3,0},{4,7},{5,6},{6,5},{7,4},{8,11},{9,10},{10,... | collective-permute-start | bytes 196616 | tf_op jit(solution)/shard_map/ppermute | solution.py:134
  87.8 1.5 %collective-permute-start.11 = (bf16[32,1024]{1,0:T(8,128)(2,1)S(1)}, bf16[32,1024]{1,0:T(8,128)(2,1)S(1)}, u32[]{:S(2)}, u32[]{:S(2)}) collective-permute-start(bf16[32,1024]{1,0:T(8,128)(2,1)S(1)} %get-tuple-element.36), channel_id=1, source_target_pairs={{0,2},{1,3},{2,0},{3,1},{4,6},{5,7},{6,4},{7,5},{8,10},{9,11},{10,... | collective-permute-start | bytes 196616 | tf_op jit(solution)/shard_map/ppermute | solution.py:134
  89.3 1.9 %collective-permute-done.10 = bf16[32,1024]{1,0:T(8,128)(2,1)S(1)} collective-permute-done((bf16[32,1024]{1,0:T(8,128)(2,1)S(1)}, bf16[32,1024]{1,0:T(8,128)(2,1)S(1)}, u32[]{:S(2)}, u32[]{:S(2)}) %collective-permute-start.10) | collective-permute-done | bytes 65568 | tf_op jit(solution)/shard_map/ppermute | solution.py:134
  91.2 0.8 collective-permute-done.12
  92.0 2.2 %collective-permute-done.11 = bf16[32,1024]{1,0:T(8,128)(2,1)S(1)} collective-permute-done((bf16[32,1024]{1,0:T(8,128)(2,1)S(1)}, bf16[32,1024]{1,0:T(8,128)(2,1)S(1)}, u32[]{:S(2)}, u32[]{:S(2)}) %collective-permute-start.11) | collective-permute-done | bytes 65568 | tf_op jit(solution)/shard_map/ppermute | solution.py:134
  94.3 2.5 %collective-permute-start.13 = (bf16[16,1024]{1,0:T(8,128)(2,1)S(1)}, bf16[16,1024]{1,0:T(8,128)(2,1)S(1)}, u32[]{:S(2)}, u32[]{:S(2)}) collective-permute-start(bf16[16,1024]{1,0:T(8,128)(2,1)S(1)} %slice.41), channel_id=1, source_target_pairs={{0,6},{1,7},{2,4},{3,5},{4,2},{5,3},{6,0},{7,1},{8,14},{9,15},{10,... | collective-permute-start | bytes 98312 | tf_op jit(solution)/shard_map/ppermute | solution.py:134
  96.8 0.0 copy-done.1
  96.8 0.0 copy-done.4
  96.8 0.0 copy-done.6
  96.8 9.0 %own_backward.1 = (bf16[256,2560]{1,0:T(8,128)(2,1)}, bf16[256,512]{1,0:T(8,128)(2,1)}, bf16[256,512]{1,0:T(8,128)(2,1)}) custom-call(bf16[256,2560]{1,0:T(8,128)(2,1)S(1)} %copy-done.1, bf16[256,2560]{1,0:T(8,128)(2,1)S(1)} %get-tuple-element.22.refs_1_, bf16[256,512]{1,0:T(8,128)(2,1)S(1)} %copy-done.4, bf16[256,512]{1,0:T(8,128)(2,1)S(1)} %copy-done.6, ...), custom_call_target="tpu_custom_call" | custom-call | flops 3355443200 | bytes 12582912 | tf_op jit(solution)/shard_map/own_backward/pallas_call | solution.py:219
  105.8 0.0 collective-permute-done.13
  105.8 0.1 reshape.29
  105.9 0.2 slice_reduce_fusion
  106.1 0.6 copy_bitcast_fusion
  (9 shorter events, 0.1 us)
Async XLA Ops:
  2.0 8.2 %collective-permute-start = (bf16[16,1152]{1,0:T(8,128)(2,1)S(1)}, bf16[16,1152]{1,0:T(8,128)(2,1)S(1)}, u32[]{:S(2)}, u32[]{:S(2)}) collective-permute-start(bf16[16,1152]{1,0:T(8,128)(2,1)S(1)} %get-tuple-element.37), channel_id=1, source_target_pairs={{0,6},{1,7},{2,4},{3,5},{4,2},{5,3},{6,0},{7,1},{8,14},{9,15},{10,... | collective-permute-start | bytes 110600 | tf_op jit(solution)/shard_map/ppermute | solution.py:134
  11.0 8.9 %collective-permute-start.3 = (bf16[32,1152]{1,0:T(8,128)(2,1)S(1)}, bf16[32,1152]{1,0:T(8,128)(2,1)S(1)}, u32[]{:S(2)}, u32[]{:S(2)}) collective-permute-start(bf16[32,1152]{1,0:T(8,128)(2,1)S(1)} %pad_maximum_fusion), channel_id=1, source_target_pairs={{0,3},{1,2},{2,1},{3,0},{4,7},{5,6},{6,5},{7,4},{8,11},{9,10},{10,... | collective-permute-start | bytes 221192 | tf_op jit(solution)/shard_map/ppermute | solution.py:134
  13.5 6.4 %collective-permute-start.2 = (bf16[32,1152]{1,0:T(8,128)(2,1)S(1)}, bf16[32,1152]{1,0:T(8,128)(2,1)S(1)}, u32[]{:S(2)}, u32[]{:S(2)}) collective-permute-start(bf16[32,1152]{1,0:T(8,128)(2,1)S(1)} %pad_maximum_fusion), channel_id=1, source_target_pairs={{0,2},{1,3},{2,0},{3,1},{4,6},{5,7},{6,4},{7,5},{8,10},{9,11},{10,... | collective-permute-start | bytes 221192 | tf_op jit(solution)/shard_map/ppermute | solution.py:134
  13.5 5.0 %collective-permute-start.1 = (bf16[32,1152]{1,0:T(8,128)(2,1)S(1)}, bf16[32,1152]{1,0:T(8,128)(2,1)S(1)}, u32[]{:S(2)}, u32[]{:S(2)}) collective-permute-start(bf16[32,1152]{1,0:T(8,128)(2,1)S(1)} %pad_maximum_fusion), channel_id=1, source_target_pairs={{0,1},{1,0},{2,3},{3,2},{4,5},{5,4},{6,7},{7,6},{8,9},{9,8},{10,11... | collective-permute-start | bytes 221192 | tf_op jit(solution)/shard_map/ppermute | solution.py:134
  19.9 16.7 %collective-permute-start.6 = (bf16[128,1152]{1,0:T(8,128)(2,1)S(1)}, bf16[128,1152]{1,0:T(8,128)(2,1)S(1)}, u32[]{:S(2)}, u32[]{:S(2)}) collective-permute-start(bf16[128,1152]{1,0:T(8,128)(2,1)S(1)} %constant_dynamic-update-slice_fusion.refs_5_.refs_6_.refs_7_), channel_id=1, source_target_pairs={{0,24},{1,25},{2,26},{3,27},{4,28},{5,29},{6,30},{7,31},{8,16},{9,... | collective-permute-start | bytes 884744 | tf_op jit(solution)/shard_map/ppermute | solution.py:134
  22.8 13.9 %collective-permute-start.5 = (bf16[128,1152]{1,0:T(8,128)(2,1)S(1)}, bf16[128,1152]{1,0:T(8,128)(2,1)S(1)}, u32[]{:S(2)}, u32[]{:S(2)}) collective-permute-start(bf16[128,1152]{1,0:T(8,128)(2,1)S(1)} %constant_dynamic-update-slice_fusion.refs_5_.refs_6_.refs_7_), channel_id=1, source_target_pairs={{0,16},{1,17},{2,18},{3,19},{4,20},{5,21},{6,22},{7,23},{8,24},{9,... | collective-permute-start | bytes 884744 | tf_op jit(solution)/shard_map/ppermute | solution.py:134
  23.6 13.1 %collective-permute-start.4 = (bf16[128,1152]{1,0:T(8,128)(2,1)S(1)}, bf16[128,1152]{1,0:T(8,128)(2,1)S(1)}, u32[]{:S(2)}, u32[]{:S(2)}) collective-permute-start(bf16[128,1152]{1,0:T(8,128)(2,1)S(1)} %constant_dynamic-update-slice_fusion.refs_5_.refs_6_.refs_7_), channel_id=1, source_target_pairs={{0,8},{1,9},{2,10},{3,11},{4,12},{5,13},{6,14},{7,15},{8,0},{9,1},... | collective-permute-start | bytes 884744 | tf_op jit(solution)/shard_map/ppermute | solution.py:134
  24.8 1.3 %copy-start = (bf16[256,2560]{1,0:T(8,128)(2,1)S(1)}, bf16[256,2560]{1,0:T(8,128)(2,1)}, u32[]{:S(2)}) copy-start(bf16[256,2560]{1,0:T(8,128)(2,1)} %refs_0_.2) | copy-start | bytes 3932164
  26.1 0.9 copy-start.3
  27.1 0.9 copy-start.5
  28.0 0.7 copy-start.7
  35.1 1.6 %copy-start.2 = (bf16[20,256,256]{2,1,0:T(8,128)(2,1)}, bf16[20,256,256]{2,1,0:T(8,128)(2,1)S(1)}, u32[]{:S(2)}) copy-start(bf16[20,256,256]{2,1,0:T(8,128)(2,1)S(1)} %get-tuple-element.23.refs_4_) | copy-start | bytes 7864324
  71.4 10.8 %collective-permute-start.7 = (bf16[128,1024]{1,0:T(8,128)(2,1)S(1)}, bf16[128,1024]{1,0:T(8,128)(2,1)S(1)}, u32[]{:S(2)}, u32[]{:S(2)}) collective-permute-start(bf16[128,1024]{1,0:T(8,128)(2,1)S(1)} %prefix_grads_2.1), channel_id=1, source_target_pairs={{0,16},{1,17},{2,18},{3,19},{4,20},{5,21},{6,22},{7,23},{8,24},{9,... | collective-permute-start | bytes 786440 | tf_op jit(solution)/shard_map/ppermute | solution.py:134
  74.5 11.0 %collective-permute-start.8 = (bf16[128,1024]{1,0:T(8,128)(2,1)S(1)}, bf16[128,1024]{1,0:T(8,128)(2,1)S(1)}, u32[]{:S(2)}, u32[]{:S(2)}) collective-permute-start(bf16[128,1024]{1,0:T(8,128)(2,1)S(1)} %prefix_grads_1.1), channel_id=1, source_target_pairs={{0,8},{1,9},{2,10},{3,11},{4,12},{5,13},{6,14},{7,15},{8,0},{9,1},... | collective-permute-start | bytes 786440 | tf_op jit(solution)/shard_map/ppermute | solution.py:134
  75.1 10.4 %collective-permute-start.9 = (bf16[128,1024]{1,0:T(8,128)(2,1)S(1)}, bf16[128,1024]{1,0:T(8,128)(2,1)S(1)}, u32[]{:S(2)}, u32[]{:S(2)}) collective-permute-start(bf16[128,1024]{1,0:T(8,128)(2,1)S(1)} %prefix_grads_3.1), channel_id=1, source_target_pairs={{0,24},{1,25},{2,26},{3,27},{4,28},{5,29},{6,30},{7,31},{8,16},{9,... | collective-permute-start | bytes 786440 | tf_op jit(solution)/shard_map/ppermute | solution.py:134
  79.1 17.6 %copy-start.1 = (bf16[256,2560]{1,0:T(8,128)(2,1)S(1)}, bf16[256,2560]{1,0:T(8,128)(2,1)}, u32[]{:S(2)}) copy-start(bf16[256,2560]{1,0:T(8,128)(2,1)} %refs_0_.2) | copy-start | bytes 3932164
  79.1 17.6 %copy-start.4 = (bf16[256,512]{1,0:T(8,128)(2,1)S(1)}, bf16[256,512]{1,0:T(8,128)(2,1)}, u32[]{:S(2)}) copy-start(bf16[256,512]{1,0:T(8,128)(2,1)} %refs_2_.5) | copy-start | bytes 786436
  79.2 17.6 %copy-start.6 = (bf16[256,512]{1,0:T(8,128)(2,1)S(1)}, bf16[256,512]{1,0:T(8,128)(2,1)}, u32[]{:S(2)}) copy-start(bf16[256,512]{1,0:T(8,128)(2,1)} %refs_3_.3) | copy-start | bytes 786436
  85.7 5.5 %collective-permute-start.10 = (bf16[32,1024]{1,0:T(8,128)(2,1)S(1)}, bf16[32,1024]{1,0:T(8,128)(2,1)S(1)}, u32[]{:S(2)}, u32[]{:S(2)}) collective-permute-start(bf16[32,1024]{1,0:T(8,128)(2,1)S(1)} %get-tuple-element.34), channel_id=1, source_target_pairs={{0,1},{1,0},{2,3},{3,2},{4,5},{5,4},{6,7},{7,6},{8,9},{9,8},{10,11... | collective-permute-start | bytes 196616 | tf_op jit(solution)/shard_map/ppermute | solution.py:134
  85.8 6.2 %collective-permute-start.12 = (bf16[32,1024]{1,0:T(8,128)(2,1)S(1)}, bf16[32,1024]{1,0:T(8,128)(2,1)S(1)}, u32[]{:S(2)}, u32[]{:S(2)}) collective-permute-start(bf16[32,1024]{1,0:T(8,128)(2,1)S(1)} %get-tuple-element.35), channel_id=1, source_target_pairs={{0,3},{1,2},{2,1},{3,0},{4,7},{5,6},{6,5},{7,4},{8,11},{9,10},{10,... | collective-permute-start | bytes 196616 | tf_op jit(solution)/shard_map/ppermute | solution.py:134
  87.8 6.5 %collective-permute-start.11 = (bf16[32,1024]{1,0:T(8,128)(2,1)S(1)}, bf16[32,1024]{1,0:T(8,128)(2,1)S(1)}, u32[]{:S(2)}, u32[]{:S(2)}) collective-permute-start(bf16[32,1024]{1,0:T(8,128)(2,1)S(1)} %get-tuple-element.36), channel_id=1, source_target_pairs={{0,2},{1,3},{2,0},{3,1},{4,6},{5,7},{6,4},{7,5},{8,10},{9,11},{10,... | collective-permute-start | bytes 196616 | tf_op jit(solution)/shard_map/ppermute | solution.py:134
  94.3 11.5 %collective-permute-start.13 = (bf16[16,1024]{1,0:T(8,128)(2,1)S(1)}, bf16[16,1024]{1,0:T(8,128)(2,1)S(1)}, u32[]{:S(2)}, u32[]{:S(2)}) collective-permute-start(bf16[16,1024]{1,0:T(8,128)(2,1)S(1)} %slice.41), channel_id=1, source_target_pairs={{0,6},{1,7},{2,4},{3,5},{4,2},{5,3},{6,0},{7,1},{8,14},{9,15},{10,... | collective-permute-start | bytes 98312 | tf_op jit(solution)/shard_map/ppermute | solution.py:134
